TPU v7x, 32 devices: a whole 2x2x4 slice. The times are simulated.
32 devices in a mesh: groups: 2 (over y), row: 16 (over z, x, core).
Axes of the slice: x: 2, y: 2, z: 4, core: 2. Of those that a mesh axis runs over, the one named last changes fastest.
Arguments:
- tokens: bfloat16 [64, 8192], P(('groups', 'row')), parts along dimension 0, may hold values from -6 to 6
- norm_gain: float32 [8192], replicated, may hold values from 0.1 to 1.9
- gate_weight: bfloat16 [8192, 26624], P(None, 'row'), may hold values from -0.0625 to 0.0625
- up_weight: bfloat16 [8192, 26624], P(None, 'row'), may hold values from -0.0625 to 0.0625
- down_weight: bfloat16 [26624, 8192], P('row'), may hold values from -0.0390625 to 0.0390625
Outputs:
- scored: bfloat16 [64, 8192], P(('groups', 'row')), parts along dimension 0
There are 2 independent parts, one for each index of `groups`. A program takes and returns all parts, laid end to end along the dimension named above; an argument that names none is the same for every part. Nothing has to cross between parts.
All inputs are finite; a program needn't handle non-finite values.
Results may differ from a plain program's by a relative error of at most 0.0065.
Values may be sent and summed in bfloat16 or wider, within the bound.
A program may use at most 192 MiB of HBM per device.

v0:
```python
import jax
import jax.numpy as jnp
from jax import lax
from jax.sharding import PartitionSpec as P

epsilon = 1e-05


def normalize(tokens, norm_gain):
    floated = tokens.astype(jnp.float32)
    mean_square = jnp.mean(floated * floated, axis=-1, keepdims=True)
    return (floated * lax.rsqrt(mean_square + epsilon) * norm_gain).astype(jnp.bfloat16)


def per_device(tokens, norm_gain, gate_weight, up_weight, down_weight):
    source = normalize(tokens, norm_gain)
    gate_out = jnp.dot(
        lax.all_gather(source, "row", axis=0, tiled=True),
        gate_weight,
        preferred_element_type=jnp.float32,
    )
    up_out = jnp.dot(
        lax.all_gather(source, "row", axis=0, tiled=True),
        up_weight,
        preferred_element_type=jnp.float32,
    )
    hidden = (jax.nn.silu(gate_out) * up_out).astype(jnp.bfloat16)
    summed = lax.psum_scatter(
        jnp.dot(hidden, down_weight, preferred_element_type=jnp.float32),
        "row",
        scatter_dimension=0,
        tiled=True,
    )
    return summed.astype(jnp.bfloat16)


def solution(mesh):
    placed = (P(("groups", "row"), None), P(), P(None, "row"), P(None, "row"), P("row", None))
    return jax.shard_map(
        per_device,
        mesh=mesh,
        in_specs=placed,
        out_specs=P(("groups", "row"), None),
        check_vma=False,
    )
```

profile of v0, /device:TPU:0, one launch (start us, length us, event | category | flops | bytes accessed | tf_op | source)
XLA Modules:
  0.0 129.6 jit_solution(11389414217199470628)
XLA Ops:
  0.0 0.9 fusion.8
  0.9 0.9 fusion.11
  1.8 24.6 %all-gather = bf16[16,2,8192]{2,1,0:T(2,128)(2,1)S(1)} all-gather(bf16[1,2,8192]{2,1,0:T(2,128)(2,1)S(1)} %fusion.11), channel_id=1, replica_groups=mesh['groups'=2,'row'=16] {'row'}, dimensions={0}, use_global_device_ids=true | all-gather | bytes 557056 | tf_op jit(solution)/shard_map/all_gather | solution.py:18
  26.4 0.2 reshape.10
  26.6 11.1 %fusion.13 = f32[32,1664]{1,0:T(8,128)S(1)} fusion(bf16[32,8192]{1,0:T(8,128)(2,1)S(1)} %reshape.10, bf16[8192,1664]{1,0:T(8,128)(2,1)} %param.7), kind=kOutput, calls=%fused_computation.18 | convolution fusion | flops 872415232 | bytes 28000256 | tf_op jit(solution)/shard_map/dot_general | solution.py:17
  37.7 0.0 copy-start
  37.8 20.4 %fusion.1 = f32[32,8192]{1,0:T(8,128)S(1)} fusion(bf16[1664,8192]{1,0:T(8,128)(2,1)} %param.9, bf16[32,8192]{1,0:T(8,128)(2,1)S(1)} %reshape.10, bf16[8192,1664]{1,0:T(8,128)(2,1)} %param.8, f32[32,1664]{1,0:T(8,128)S(1)} %fusion.13), kind=kOutput, calls=%fused_computation.2 | convolution fusion | flops 1745149952 | bytes 56311808 | tf_op jit(solution)/shard_map/dot_general | solution.py:29
  58.2 69.5 %all-reduce.2 = bf16[32,8192]{1,0:T(8,128)(2,1)S(1)} all-reduce(f32[32,8192]{1,0:T(8,128)S(1)} %fusion.1), channel_id=2, replica_groups=mesh['groups'=2,'row'=16] {'row'}, use_global_device_ids=true, to_apply=%region_1.2.clone | all-reduce | flops 262144 | bytes 1572864
  127.7 0.0 copy-done
  127.7 0.6 dynamic-slice
  129.0 0.7 dynamic-slice_convert_fusion
  (1 shorter events, 0.0 us)
Async XLA Ops:
  37.7 90.0 %copy-start = (u32[32]{0:T(128)S(1)}, u32[32]{0:T(128)}, u32[]{:S(2)}) copy-start(u32[32]{0:T(128)} %constant.13) | copy-start | bytes 388
where the time goes:
time: 130 us
  blocking collectives  94.1 us (72%)
  matrix products  31.5 us (24%)
  other arithmetic  1.83 us (1%)
  local copies, waits for them, and re-layouts  1.44 us (1%)
    unnamed x1, blocking collectives  69.5 us
    all_gather x1, blocking collectives, per_device(): lax.all_gather(source, 'row', axis=0, tiled=True)  24.6 us
    dot_general x1, matrix products, per_device(): jnp.dot(hidden, down_weight, preferred_element_type=jnp.float32)  20.4 us
    dot_general x1, matrix products, per_device(): jnp.dot(lax.all_gather(source, 'row', axis=0, tiled=True), gate_weight, p...  11.1 us

commit v1 on v0

v1 whole, which is shorter than its diff:
```python
import functools

import jax
import jax.numpy as jnp
from jax import lax
from jax.experimental import pallas as pl
from jax.experimental.pallas import tpu as pltpu
from jax.sharding import PartitionSpec as P

epsilon = 1e-05
LANES = 128
K_CHUNK = 512
N_CHUNK = 1024
RING = 22
DOWN_RING = 4
MESH = pl.DeviceIdType.MESH


def whole_wait(ref, sem):
    pltpu.make_async_copy(ref, ref, sem).wait()


def kernel(
    chips,
    tokens_hbm,
    gain_hbm,
    gate_hbm,
    up_hbm,
    down_hbm,
    out_ref,
    tokens,
    gain,
    spread,
    piece,
    gathered,
    gathered_f32,
    x,
    ring,
    down_ring,
    gate_acc,
    up_acc,
    hidden,
    partial,
    mine,
    sib_send,
    sib_recv,
    chip_send,
    chip_recv,
    total,
    in_sem,
    ring_sem,
    down_sem,
    ag_send_sem,
    ag_recv_sem,
    fwd_send_sem,
    fwd_recv_sem,
    sib_send_sem,
    sib_recv_sem,
    chip_send_sem,
    chip_recv_sem,
):
    own, features = tokens.shape
    slots = ring.shape[0]
    down_slots = down_ring.shape[0]
    k_steps = features // K_CHUNK
    n_steps = features // N_CHUNK
    folds = features // LANES
    chunk_folds = N_CHUNK // LANES
    rows = 2 * chips * own
    half = chips * own * chunk_folds

    group = lax.axis_index("groups")
    me = lax.axis_index("row")
    core = lax.rem(me, 2)
    chip = me // 2
    other = 1 - core

    def at(to_chip, to_core):
        return (group, 2 * to_chip + to_core)

    def peer(step):
        return lax.rem(chip + step, chips)

    def gate_up_copy(index, hbm, step, slot):
        return pltpu.make_async_copy(
            hbm.at[pl.ds(pl.multiple_of(step * K_CHUNK, K_CHUNK), K_CHUNK)],
            ring.at[slot],
            ring_sem.at[slot],
        )

    def start_weight(index):
        step, slot = index // 2, lax.rem(index, slots)

        @pl.when(lax.rem(index, 2) == 0)
        def _():
            gate_up_copy(index, gate_hbm, step, slot).start()

        @pl.when(lax.rem(index, 2) == 1)
        def _():
            gate_up_copy(index, up_hbm, step, slot).start()

    def down_copy(step):
        slot = lax.rem(step, down_slots)
        return pltpu.make_async_copy(
            down_hbm.at[:, pl.ds(pl.multiple_of(step * N_CHUNK, N_CHUNK), N_CHUNK)],
            down_ring.at[slot],
            down_sem.at[slot],
        )

    tokens_in = pltpu.make_async_copy(tokens_hbm, tokens, in_sem.at[0])
    gain_in = pltpu.make_async_copy(gain_hbm, gain, in_sem.at[1])
    tokens_in.start()
    gain_in.start()
    barrier = pltpu.get_barrier_semaphore()

    def greet(step, carry):
        pl.semaphore_signal(barrier, inc=1, device_id=at(peer(step), core), device_id_type=MESH)
        return carry

    pl.semaphore_signal(barrier, inc=1, device_id=at(chip, other), device_id_type=MESH)
    lax.fori_loop(1, chips, greet, 0)
    for index in range(slots):
        gate_up_copy(index, (gate_hbm, up_hbm)[index % 2], index // 2, index % slots).start()

    tokens_in.wait()
    gain_in.wait()
    floated = tokens[...].astype(jnp.float32)
    mean_square = jnp.mean(floated * floated, axis=-1, keepdims=True)
    normed = floated * lax.rsqrt(mean_square + epsilon) * gain[...]
    for fold in range(folds):
        spread[pl.ds(fold, own, stride=folds), :] = normed[:, fold * LANES : (fold + 1) * LANES]
    piece[...] = spread[...].astype(jnp.bfloat16)
    gathered[core, chip] = piece[...]
    pl.semaphore_wait(barrier, chips)

    def forward(which):
        return pltpu.make_async_remote_copy(
            src_ref=gathered.at[core, which],
            dst_ref=gathered.at[core, which],
            send_sem=fwd_send_sem,
            recv_sem=fwd_recv_sem,
            device_id=at(chip, other),
            device_id_type=MESH,
        )

    def announce(step, carry):
        pltpu.make_async_remote_copy(
            src_ref=piece,
            dst_ref=gathered.at[core, chip],
            send_sem=ag_send_sem,
            recv_sem=ag_recv_sem.at[chip],
            device_id=at(peer(step), core),
            device_id_type=MESH,
        ).start()
        return carry

    lax.fori_loop(1, chips, announce, 0)
    forward(chip).start()

    def pass_on(step, carry):
        which = peer(step)
        whole_wait(gathered.at[core, which], ag_recv_sem.at[which])
        forward(which).start()
        return carry

    lax.fori_loop(1, chips, pass_on, 0)
    whole_wait(gathered.at[other], fwd_recv_sem)

    gathered_f32[...] = gathered[...].astype(jnp.float32).reshape(gathered_f32.shape)
    per_step = K_CHUNK // LANES
    for fold in range(folds):
        x[fold // per_step, :, (fold % per_step) * LANES : (fold % per_step + 1) * LANES] = gathered_f32[
            pl.ds(fold, rows, stride=folds), :
        ].astype(jnp.bfloat16)
    gate_acc[...] = jnp.zeros_like(gate_acc)
    up_acc[...] = jnp.zeros_like(up_acc)

    def refill(index):
        @pl.when(index + slots < 2 * k_steps)
        def _():
            start_weight(index + slots)

        ahead = index + slots - 2 * k_steps

        @pl.when(jnp.logical_and(ahead >= 0, ahead < down_slots))
        def _():
            down_copy(ahead).start()

    def project(step, carry):
        for part, (hbm, acc) in enumerate(((gate_hbm, gate_acc), (up_hbm, up_acc))):
            index = 2 * step + part
            slot = lax.rem(index, slots)
            gate_up_copy(index, hbm, step, slot).wait()
            acc[...] += jnp.dot(x[step], ring[slot], preferred_element_type=jnp.float32)
            refill(index)
        return carry

    lax.fori_loop(0, k_steps, project, 0)
    gate_out = gate_acc[...]
    hidden[...] = (gate_out / (1.0 + jnp.exp(-gate_out)) * up_acc[...]).astype(jnp.bfloat16)

    def sibling(step):
        return pltpu.make_async_remote_copy(
            src_ref=sib_send.at[step],
            dst_ref=sib_recv.at[step],
            send_sem=sib_send_sem.at[step],
            recv_sem=sib_recv_sem.at[step],
            device_id=at(chip, other),
            device_id_type=MESH,
        )

    def produce(step):
        slot = lax.rem(step, down_slots)
        down_copy(step).wait()
        product = jnp.dot(hidden[...], down_ring[slot], preferred_element_type=jnp.float32)
        for fold in range(chunk_folds):
            partial[pl.ds(fold, rows, stride=chunk_folds), :] = product[:, fold * LANES : (fold + 1) * LANES]
        sib_send[step] = partial[pl.ds(pl.multiple_of(other * half, half), half), :].astype(jnp.bfloat16)
        mine[step] = partial[pl.ds(pl.multiple_of(core * half, half), half), :]
        sibling(step).start()

        @pl.when(step + down_slots < n_steps)
        def _():
            down_copy(step + down_slots).start()

    def exchange(step):
        sibling(step).wait_recv()
        both = mine[step] + sib_recv[step].astype(jnp.float32)
        chip_send[step] = both.astype(jnp.bfloat16).reshape(chip_send.shape[1:])

        def send(ahead, carry):
            to = peer(ahead)
            pltpu.make_async_remote_copy(
                src_ref=chip_send.at[step, to],
                dst_ref=chip_recv.at[step, chip],
                send_sem=chip_send_sem.at[step],
                recv_sem=chip_recv_sem.at[step],
                device_id=at(to, core),
                device_id_type=MESH,
            ).start()
            return carry

        lax.fori_loop(1, chips, send, 0)
        chip_recv[step, chip] = chip_send[step, chip]

    def finish(step):
        whole_wait(chip_recv.at[step, pl.ds(0, chips - 1)], chip_recv_sem.at[step])
        total[...] = jnp.sum(chip_recv[step].astype(jnp.float32), axis=0)
        for fold in range(chunk_folds):
            out_ref[:, pl.ds(pl.multiple_of(step * N_CHUNK, N_CHUNK) + fold * LANES, LANES)] = total[
                pl.ds(fold, own, stride=chunk_folds), :
            ].astype(jnp.bfloat16)

    def score(step, carry):
        produce(step)

        @pl.when(step >= 1)
        def _():
            exchange(step - 1)

        return carry

    lax.fori_loop(0, n_steps, score, 0)
    exchange(n_steps - 1)

    def close(step, carry):
        finish(step)
        return carry

    lax.fori_loop(0, n_steps, close, 0)

    def drain(step, carry):
        sibling(step).wait_send()
        whole_wait(chip_send.at[step, pl.ds(0, chips - 1)], chip_send_sem.at[step])
        return carry

    lax.fori_loop(0, n_steps, drain, 0)
    whole_wait(gathered.at[core, pl.ds(0, chips - 1)], ag_send_sem)
    whole_wait(gathered.at[core], fwd_send_sem)


def per_device(devices, tokens, norm_gain, gate_weight, up_weight, down_weight):
    own, features = tokens.shape
    units = gate_weight.shape[1]
    chips = devices // 2
    rows = devices * own
    folds = features // LANES
    k_steps, n_steps = features // K_CHUNK, features // N_CHUNK
    chunk_folds = N_CHUNK // LANES
    half = chips * own * chunk_folds
    slots, down_slots = min(RING, 2 * k_steps), min(DOWN_RING, n_steps)
    bf16, f32 = jnp.bfloat16, jnp.float32
    dma = pltpu.SemaphoreType.DMA
    return pl.pallas_call(
        functools.partial(kernel, chips),
        out_shape=jax.ShapeDtypeStruct((own, features), bf16),
        in_specs=[pl.BlockSpec(memory_space=pl.ANY)] * 5,
        out_specs=pl.BlockSpec(memory_space=pltpu.VMEM),
        scratch_shapes=[
            pltpu.VMEM((own, features), bf16),
            pltpu.VMEM((1, features), f32),
            pltpu.VMEM((own * folds, LANES), f32),
            pltpu.VMEM((own * folds, LANES), bf16),
            pltpu.VMEM((2, chips, own * folds, LANES), bf16),
            pltpu.VMEM((rows * folds, LANES), f32),
            pltpu.VMEM((k_steps, rows, K_CHUNK), bf16),
            pltpu.VMEM((slots, K_CHUNK, units), bf16),
            pltpu.VMEM((down_slots, units, N_CHUNK), bf16),
            pltpu.VMEM((rows, units), f32),
            pltpu.VMEM((rows, units), f32),
            pltpu.VMEM((rows, units), bf16),
            pltpu.VMEM((rows * chunk_folds, LANES), f32),
            pltpu.VMEM((n_steps, half, LANES), f32),
            pltpu.VMEM((n_steps, half, LANES), bf16),
            pltpu.VMEM((n_steps, half, LANES), bf16),
            pltpu.VMEM((n_steps, chips, own * chunk_folds, LANES), bf16),
            pltpu.VMEM((n_steps, chips, own * chunk_folds, LANES), bf16),
            pltpu.VMEM((own * chunk_folds, LANES), f32),
            dma((2,)),
            dma((slots,)),
            dma((down_slots,)),
            dma,
            dma((chips,)),
            dma,
            dma,
            dma((n_steps,)),
            dma((n_steps,)),
            dma((n_steps,)),
            dma((n_steps,)),
        ],
        compiler_params=pltpu.CompilerParams(
            collective_id=0, has_side_effects=True, vmem_limit_bytes=60 * 1024 * 1024
        ),
        cost_estimate=pl.CostEstimate(
            flops=6 * rows * features * units,
            bytes_accessed=6 * features * units,
            transcendentals=rows * units,
        ),
    )(tokens, norm_gain.reshape(1, features), gate_weight, up_weight, down_weight)


def solution(mesh):
    placed = (P(("groups", "row"), None), P(), P(None, "row"), P(None, "row"), P("row", None))
    return jax.shard_map(
        functools.partial(per_device, mesh.shape["row"]),
        mesh=mesh,
        in_specs=placed,
        out_specs=P(("groups", "row"), None),
        check_vma=False,
    )
```

time: 130 us -> 42.9 us (0.33)
  blocking collectives: 94.1 us -> 0 us
  Pallas kernels: 0 us -> 41.3 us
  matrix products: 31.5 us -> 0 us
  other arithmetic: 1.83 us -> 0 us
    unnamed x1 -> x0, blocking collectives: 69.5 us -> none
    pallas_call x0 -> x1, Pallas kernels: none -> 41.3 us  [per_device(): pl.pallas_call(functools.partial(kernel, chips), out_shape=jax.ShapeDtype...]
    dot_general x2 -> x0, matrix products: 31.5 us -> none  [the longest x1 20.4 us: per_device(): jnp.dot(hidden, down_weight, preferred_element_type=jnp.float32)]
    all_gather x1 -> x0, blocking collectives: 24.6 us -> none  [per_device(): lax.all_gather(source, 'row', axis=0, tiled=True)]
where the time goes in v1:
time: 42.9 us; the launch traced here: 42.7 us
  Pallas kernels  41.3 us (96%)
  local copies, waits for them, and re-layouts  1.4 us (3%)
    pallas_call x1, Pallas kernels, per_device(): pl.pallas_call(functools.partial(kernel, chips), out_shape=jax.ShapeDtype...  41.3 us
    unnamed x1, local copies, waits for them, and re-layouts  1.4 us

profile of v1, /device:TPU:0, one launch (start us, length us, event | category | flops | bytes accessed | tf_op | source)
XLA Modules:
  0.0 42.7 jit_solution(3991012876573998843)
XLA Ops:
  0.0 41.3 %shard_map.55 = bf16[2,8192]{1,0:T(2,128)(2,1)} custom-call(bf16[2,8192]{1,0:T(2,128)(2,1)} %tokens_hbm.1, f32[1,8192]{1,0:T(1,128)} %bitcast.1, bf16[8192,1664]{1,0:T(8,128)(2,1)} %gate_hbm.1, bf16[8192,1664]{1,0:T(8,128)(2,1)} %up_hbm.1, bf16[1664,8192]{1,0:T(8,128)(2,1)} %down_hbm.1), custom_call_target="tpu_custom_call" | custom-call | flops 2617245696 | bytes 81788928 | tf_op jit(solution)/shard_map/pallas_call | solution.py:294
  41.3 1.4 %copy.7 = bf16[2,8192]{1,0:T(2,128)(2,1)} copy(bf16[2,8192]{1,0:T(2,128)(2,1)} %shard_map.55) | data formatting | bytes 65536

commit v2 on v0

v2 whole, which is shorter than its diff:
```python
import functools

import jax
import jax.numpy as jnp
from jax import lax
from jax.experimental import pallas as pl
from jax.experimental.pallas import tpu as pltpu
from jax.sharding import PartitionSpec as P

epsilon = 1e-05
LANES = 128
TILE = 256
K_CHUNK = 1024
N_CHUNK = 1024
RING = 6
DOWN_RING = 4
PIECES = 4
WIDE = 2
MESH = pl.DeviceIdType.MESH


def whole_wait(ref, sem):
    pltpu.make_async_copy(ref, ref, sem).wait()


def each(start, stop, body):
    if stop - start <= 8:
        for step in range(start, stop):
            body(step)
    else:
        pl.loop(start, stop)(body)


def kernel(
    chips,
    tokens_hbm,
    gain_hbm,
    gate_hbm,
    up_hbm,
    down_hbm,
    out_ref,
    tokens,
    gain,
    spread,
    piece,
    gathered,
    gathered_f32,
    x,
    ring,
    down_ring,
    acc,
    hidden,
    in_sem,
    ring_sem,
    down_sem,
    ag_send_sem,
    ag_recv_sem,
    fwd_send_sem,
    fwd_recv_sem,
    *groups,
):
    own, features = tokens.shape
    units = gate_hbm.shape[1]
    slots, parts, _, width = ring.shape
    down_slots = down_ring.shape[0]
    k_steps = features // K_CHUNK
    n_steps = features // N_CHUNK
    pieces = spread.shape[0]
    folds = features // LANES // pieces
    per_step = K_CHUNK // LANES
    rows = 2 * chips * own
    groups = [groups[first : first + 10] for first in range(0, len(groups), 10)]

    group = lax.axis_index("groups")
    me = lax.axis_index("row")
    core = lax.rem(me, 2)
    chip = me // 2
    other = 1 - core

    def at(to_chip, to_core):
        return (group, 2 * to_chip + to_core)

    def peer(step):
        return lax.rem(chip + step, chips)

    barrier = pltpu.get_barrier_semaphore()
    pl.semaphore_signal(barrier, inc=1, device_id=at(chip, other), device_id_type=MESH)
    each(
        1,
        chips,
        lambda step: pl.semaphore_signal(barrier, inc=1, device_id=at(peer(step), core), device_id_type=MESH),
    )
    tokens_in = pltpu.make_async_copy(tokens_hbm, tokens, in_sem.at[0])
    gain_in = pltpu.make_async_copy(gain_hbm, gain, in_sem.at[1])
    tokens_in.start()
    gain_in.start()

    def weight_copy(step, part):
        slot = step % slots
        if parts == 1:
            to = ring.at[slot, 0, :, pl.ds(part * units, units)]
        else:
            to = ring.at[slot, part]
        return pltpu.make_async_copy(
            (gate_hbm, up_hbm)[part].at[pl.ds(step * K_CHUNK, K_CHUNK)], to, ring_sem.at[slot, part]
        )

    def down_copy(step):
        slot = step % down_slots
        return pltpu.make_async_copy(
            down_hbm.at[:, pl.ds(step * N_CHUNK, N_CHUNK)], down_ring.at[slot], down_sem.at[slot]
        )

    for step in range(slots):
        for part in range(2):
            weight_copy(step, part).start()

    tokens_in.wait()
    gain_in.wait()
    floated = tokens[...].astype(jnp.float32)
    mean_square = jnp.mean(floated * floated, axis=-1, keepdims=True)
    normed = floated * lax.rsqrt(mean_square + epsilon) * gain[...]
    for part in range(pieces):
        for fold in range(folds):
            column = (part * folds + fold) * LANES
            spread[part, pl.ds(fold, own, stride=folds), :] = normed[:, column : column + LANES]
    piece[...] = spread[...].astype(jnp.bfloat16)
    for part in range(pieces):
        gathered[core, part, chip] = piece[part]
    pl.semaphore_wait(barrier, chips)

    def announce(part, step):
        pltpu.make_async_remote_copy(
            src_ref=piece.at[part],
            dst_ref=gathered.at[core, part, chip],
            send_sem=ag_send_sem,
            recv_sem=ag_recv_sem.at[part],
            device_id=at(peer(step), core),
            device_id_type=MESH,
        ).start()

    def forward(part):
        return pltpu.make_async_remote_copy(
            src_ref=gathered.at[core, part],
            dst_ref=gathered.at[core, part],
            send_sem=fwd_send_sem.at[part],
            recv_sem=fwd_recv_sem.at[part],
            device_id=at(chip, other),
            device_id_type=MESH,
        )

    def collect(part):
        whole_wait(gathered.at[core, part, pl.ds(0, chips - 1)], ag_recv_sem.at[part])
        forward(part).start()

    def assemble(part):
        forward(part).wait_recv()
        gathered_f32[...] = gathered[:, part].astype(jnp.float32).reshape(gathered_f32.shape)
        for fold in range(folds):
            place = part * folds + fold
            x[place // per_step, :, pl.ds(place % per_step * LANES, LANES)] = gathered_f32[
                pl.ds(fold, rows, stride=folds), :
            ].astype(jnp.bfloat16)

    def project(step):
        slot = step % slots
        for part in range(2):
            weight_copy(step, part).wait()
        for part in range(parts):
            for column in range(0, width, TILE):
                stop = min(column + TILE, width)
                product = jnp.dot(x[step], ring[slot, part, :, column:stop], preferred_element_type=jnp.float32)
                if step == 0:
                    acc[part, :, column:stop] = product
                else:
                    acc[part, :, column:stop] += product
        if step + slots < k_steps:
            for part in range(2):
                weight_copy(step + slots, part).start()
        ahead = step + slots - k_steps
        if 0 <= ahead < down_slots:
            down_copy(ahead).start()

    for part in range(pieces):
        each(1, chips, functools.partial(announce, part))
    collect(0)
    for part in range(pieces):
        assemble(part)
        steps = range(part * k_steps // pieces, (part + 1) * k_steps // pieces)
        for step in steps:
            project(step)
            if step == steps[0] and part + 1 < pieces:
                collect(part + 1)
    for ahead in range(max(0, min(slots, down_slots)), down_slots):
        down_copy(ahead).start()

    if parts == 1:
        gate_out, up_out = acc[0, :, :units], acc[0, :, units:]
    else:
        gate_out, up_out = acc[0], acc[1]
    hidden[...] = (gate_out / (1.0 + jnp.exp(-gate_out)) * up_out).astype(jnp.bfloat16)

    def sibling(part):
        _, _, sib_send, sib_recv, _, _, send_sem, recv_sem, _, _ = groups[part]
        return pltpu.make_async_remote_copy(
            src_ref=sib_send,
            dst_ref=sib_recv,
            send_sem=send_sem,
            recv_sem=recv_sem,
            device_id=at(chip, other),
            device_id_type=MESH,
        )

    def produce(part, first):
        partial, mine, sib_send = groups[part][:3]
        half = mine.shape[0]
        span = partial.shape[0] // rows
        chunks = span * LANES // N_CHUNK
        for chunk in range(chunks):
            step = first + chunk
            down_copy(step).wait()
            for column in range(0, N_CHUNK, TILE):
                product = jnp.dot(
                    hidden[...],
                    down_ring[step % down_slots, :, column : column + TILE],
                    preferred_element_type=jnp.float32,
                )
                for lane in range(0, TILE, LANES):
                    fold = (chunk * N_CHUNK + column + lane) // LANES
                    partial[pl.ds(fold, rows, stride=span), :] = product[:, lane : lane + LANES]
            if step + down_slots < n_steps:
                down_copy(step + down_slots).start()
        sib_send[...] = partial[pl.ds(pl.multiple_of(other * half, half), half), :].astype(jnp.bfloat16)
        mine[...] = partial[pl.ds(pl.multiple_of(core * half, half), half), :]
        sibling(part).start()
        return first + chunks

    def exchange(part):
        _, mine, _, sib_recv, chip_send, chip_recv, _, _, send_sem, recv_sem = groups[part]
        sibling(part).wait_recv()
        both = mine[...] + sib_recv[...].astype(jnp.float32)
        chip_send[...] = both.astype(jnp.bfloat16).reshape(chip_send.shape)

        def send(ahead):
            to = peer(ahead)
            pltpu.make_async_remote_copy(
                src_ref=chip_send.at[to],
                dst_ref=chip_recv.at[chip],
                send_sem=send_sem,
                recv_sem=recv_sem,
                device_id=at(to, core),
                device_id_type=MESH,
            ).start()

        each(1, chips, send)
        chip_recv[chip] = chip_send[chip]

    def finish(part, first):
        mine, chip_recv, recv_sem = groups[part][1], groups[part][5], groups[part][9]
        whole_wait(chip_recv.at[pl.ds(0, chips - 1)], recv_sem)
        count = chip_recv.shape[1]
        mine[pl.ds(0, count), :] = jnp.sum(chip_recv[...].astype(jnp.float32), axis=0)
        span = count // own
        for fold in range(span):
            out_ref[:, pl.ds(first * N_CHUNK + fold * LANES, LANES)] = mine[
                pl.ds(fold, own, stride=span), :
            ].astype(jnp.bfloat16)

    firsts = [0]
    last = len(groups) - 1
    for part in range(last + 1):
        firsts.append(produce(part, firsts[-1]))
        if part >= 1:
            exchange(part - 1)
    for part in range(last - 1):
        finish(part, firsts[part])
    exchange(last)
    for part in range(max(0, last - 1), last + 1):
        finish(part, firsts[part])

    for part in range(last + 1):
        sibling(part).wait_send()
        whole_wait(groups[part][4].at[pl.ds(0, chips - 1)], groups[part][8])
    for part in range(pieces):
        forward(part).wait_send()
        whole_wait(gathered.at[core, part, pl.ds(0, chips - 1)], ag_send_sem)


def per_device(devices, tokens, norm_gain, gate_weight, up_weight, down_weight):
    own, features = tokens.shape
    units = gate_weight.shape[1]
    chips = devices // 2
    rows = devices * own
    folds = features // LANES // PIECES
    k_steps, n_steps = features // K_CHUNK, features // N_CHUNK
    slots, down_slots = min(RING, k_steps), min(DOWN_RING, n_steps)
    parts = 1 if units % LANES == 0 else 2
    width = 2 * units // parts
    bf16, f32 = jnp.bfloat16, jnp.float32
    dma = pltpu.SemaphoreType.DMA
    wide = (n_steps - 2) // WIDE
    chunks = [WIDE] * wide + [1] * (n_steps - WIDE * wide)
    groups = []
    for count in chunks:
        span = count * N_CHUNK // LANES
        half = chips * own * span
        groups += [
            pltpu.VMEM((rows * span, LANES), f32),
            pltpu.VMEM((half, LANES), f32),
            pltpu.VMEM((half, LANES), bf16),
            pltpu.VMEM((half, LANES), bf16),
            pltpu.VMEM((chips, own * span, LANES), bf16),
            pltpu.VMEM((chips, own * span, LANES), bf16),
            dma,
            dma,
            dma,
            dma,
        ]
    return pl.pallas_call(
        functools.partial(kernel, chips),
        out_shape=jax.ShapeDtypeStruct((own, features), bf16),
        in_specs=[pl.BlockSpec(memory_space=pl.ANY)] * 5,
        out_specs=pl.BlockSpec(memory_space=pltpu.VMEM),
        scratch_shapes=[
            pltpu.VMEM((own, features), bf16),
            pltpu.VMEM((1, features), f32),
            pltpu.VMEM((PIECES, own * folds, LANES), f32),
            pltpu.VMEM((PIECES, own * folds, LANES), bf16),
            pltpu.VMEM((2, PIECES, chips, own * folds, LANES), bf16),
            pltpu.VMEM((rows * folds, LANES), f32),
            pltpu.VMEM((k_steps, rows, K_CHUNK), bf16),
            pltpu.VMEM((slots, parts, K_CHUNK, width), bf16),
            pltpu.VMEM((down_slots, units, N_CHUNK), bf16),
            pltpu.VMEM((parts, rows, width), f32),
            pltpu.VMEM((rows, units), bf16),
            dma((2,)),
            dma((slots, 2)),
            dma((down_slots,)),
            dma,
            dma((PIECES,)),
            dma((PIECES,)),
            dma((PIECES,)),
            *groups,
        ],
        compiler_params=pltpu.CompilerParams(
            collective_id=0, has_side_effects=True, vmem_limit_bytes=60 * 1024 * 1024
        ),
        cost_estimate=pl.CostEstimate(
            flops=6 * rows * features * units,
            bytes_accessed=6 * features * units,
            transcendentals=rows * units,
        ),
    )(tokens, norm_gain.reshape(1, features), gate_weight, up_weight, down_weight)


def solution(mesh):
    placed = (P(("groups", "row"), None), P(), P(None, "row"), P(None, "row"), P("row", None))
    return jax.shard_map(
        functools.partial(per_device, mesh.shape["row"]),
        mesh=mesh,
        in_specs=placed,
        out_specs=P(("groups", "row"), None),
        check_vma=False,
    )
```

time: 130 us -> 47.7 us (0.37)
  blocking collectives: 94.1 us -> 0 us
  Pallas kernels: 0 us -> 46.1 us
  matrix products: 31.5 us -> 0 us
  other arithmetic: 1.83 us -> 0 us
    unnamed x1 -> x0, blocking collectives: 69.5 us -> none
    pallas_call x0 -> x1, Pallas kernels: none -> 46.1 us  [per_device(): pl.pallas_call(functools.partial(kernel, chips), out_shape=jax.ShapeDtype...]
    dot_general x2 -> x0, matrix products: 31.5 us -> none  [the longest x1 20.4 us: per_device(): jnp.dot(hidden, down_weight, preferred_element_type=jnp.float32)]
    all_gather x1 -> x0, blocking collectives: 24.6 us -> none  [per_device(): lax.all_gather(source, 'row', axis=0, tiled=True)]
where the time goes in v2:
time: 47.7 us; the launch traced here: 47.5 us
  Pallas kernels  46.1 us (97%)
  local copies, waits for them, and re-layouts  1.4 us (3%)
    pallas_call x1, Pallas kernels, per_device(): pl.pallas_call(functools.partial(kernel, chips), out_shape=jax.ShapeDtype...  46.1 us
    unnamed x1, local copies, waits for them, and re-layouts  1.4 us

profile of v2, /device:TPU:0, one launch (start us, length us, event | category | flops | bytes accessed | tf_op | source)
XLA Modules:
  0.0 47.5 jit_solution(2260275202522210982)
XLA Ops:
  0.0 46.1 %shard_map.55 = bf16[2,8192]{1,0:T(2,128)(2,1)} custom-call(bf16[2,8192]{1,0:T(2,128)(2,1)} %tokens_hbm.1, f32[1,8192]{1,0:T(1,128)} %bitcast.1, bf16[8192,1664]{1,0:T(8,128)(2,1)} %gate_hbm.1, bf16[8192,1664]{1,0:T(8,128)(2,1)} %up_hbm.1, bf16[1664,8192]{1,0:T(8,128)(2,1)} %down_hbm.1), custom_call_target="tpu_custom_call" | custom-call | flops 2617245696 | bytes 81788928 | tf_op jit(solution)/shard_map/pallas_call | solution.py:319
  46.1 1.4 %copy.7 = bf16[2,8192]{1,0:T(2,128)(2,1)} copy(bf16[2,8192]{1,0:T(2,128)(2,1)} %shard_map.55) | data formatting | bytes 65536

commit v3 on v2

v3 whole, which is shorter than its diff:
```python
import functools

import jax
import jax.numpy as jnp
from jax import lax
from jax.experimental import pallas as pl
from jax.experimental.pallas import tpu as pltpu
from jax.sharding import PartitionSpec as P

epsilon = 1e-05
LANES = 128
TILE = 256
K_CHUNK = 1024
N_CHUNK = 2048
RING = 6
DOWN_RING = 4
D_CHUNK = 1024
PIECES = 4
LAG = 3
EARLY = 0
MESH = pl.DeviceIdType.MESH


def whole_wait(ref, sem):
    pltpu.make_async_copy(ref, ref, sem).wait()


def each(start, stop, body):
    pl.loop(start, stop)(body)


def kernel(
    chips,
    tokens_hbm,
    gain_hbm,
    gate_hbm,
    up_hbm,
    down_hbm,
    out_ref,
    tokens,
    gain,
    spread,
    piece,
    gathered,
    gathered_f32,
    x,
    ring,
    down_ring,
    acc,
    hidden,
    in_sem,
    ring_sem,
    down_sem,
    ag_send_sem,
    ag_recv_sem,
    fwd_send_sem,
    fwd_recv_sem,
    partial,
    mine,
    sib_send,
    sib_recv,
    chip_send,
    chip_recv,
    total,
    sib_send_sem,
    sib_recv_sem,
    chip_send_sem,
    chip_recv_sem,
):
    own, features = tokens.shape
    units = gate_hbm.shape[1]
    slots, parts, _, width = ring.shape
    down_slots = down_ring.shape[0]
    k_steps = features // K_CHUNK
    n_steps = features // N_CHUNK
    pieces = spread.shape[0]
    folds = features // LANES // pieces
    per_step = K_CHUNK // LANES
    rows = 2 * chips * own
    per_piece = k_steps // pieces
    fan = max(1, min(2, down_slots))
    subs, d_steps = N_CHUNK // D_CHUNK, features // D_CHUNK
    half, span = mine.shape[1], N_CHUNK // LANES
    group = lax.axis_index("groups")
    me = lax.axis_index("row")
    core = lax.rem(me, 2)
    chip = me // 2
    other = 1 - core

    def at(to_chip, to_core):
        return (group, 2 * to_chip + to_core)

    def peer(step):
        return lax.rem(chip + step, chips)

    barrier = pltpu.get_barrier_semaphore()
    pl.semaphore_signal(barrier, inc=1, device_id=at(chip, other), device_id_type=MESH)
    each(
        1,
        chips,
        lambda step: pl.semaphore_signal(barrier, inc=1, device_id=at(peer(step), core), device_id_type=MESH),
    )
    tokens_in = pltpu.make_async_copy(tokens_hbm, tokens, in_sem.at[0])
    gain_in = pltpu.make_async_copy(gain_hbm, gain, in_sem.at[1])
    tokens_in.start()
    gain_in.start()

    def weight_copy(step, part):
        slot = lax.rem(step, slots)
        if parts == 1:
            to = ring.at[slot, 0, :, pl.ds(part * units, units)]
        else:
            to = ring.at[slot, part]
        return pltpu.make_async_copy(
            (gate_hbm, up_hbm)[part].at[pl.ds(pl.multiple_of(step * K_CHUNK, K_CHUNK), K_CHUNK)],
            to,
            ring_sem.at[slot, part],
        )

    def down_copy(step):
        slot = lax.rem(step, down_slots)
        return pltpu.make_async_copy(
            down_hbm.at[:, pl.ds(pl.multiple_of(step * D_CHUNK, D_CHUNK), D_CHUNK)],
            down_ring.at[slot],
            down_sem.at[slot],
        )

    def fill(step):
        for part in range(2):
            weight_copy(step, part).start()

    each(0, slots, fill)

    tokens_in.wait()
    gain_in.wait()
    floated = tokens[...].astype(jnp.float32)
    mean_square = jnp.mean(floated * floated, axis=-1, keepdims=True)
    normed = floated * lax.rsqrt(mean_square + epsilon) * gain[...]
    for part in range(pieces):
        for fold in range(folds):
            column = (part * folds + fold) * LANES
            spread[part, pl.ds(fold, own, stride=folds), :] = normed[:, column : column + LANES]
    piece[...] = spread[...].astype(jnp.bfloat16)
    for part in range(pieces):
        gathered[core, part, chip] = piece[part]
    pl.semaphore_wait(barrier, chips)

    def announce(part, step):
        pltpu.make_async_remote_copy(
            src_ref=piece.at[part],
            dst_ref=gathered.at[core, part, chip],
            send_sem=ag_send_sem,
            recv_sem=ag_recv_sem.at[part],
            device_id=at(peer(step), core),
            device_id_type=MESH,
        ).start()

    def forward(part):
        return pltpu.make_async_remote_copy(
            src_ref=gathered.at[core, part],
            dst_ref=gathered.at[core, part],
            send_sem=fwd_send_sem.at[part],
            recv_sem=fwd_recv_sem.at[part],
            device_id=at(chip, other),
            device_id_type=MESH,
        )

    def collect(part):
        whole_wait(gathered.at[core, part, pl.ds(0, chips - 1)], ag_recv_sem.at[part])
        forward(part).start()

    def assemble(part):
        forward(part).wait_recv()
        gathered_f32[...] = gathered[:, part].astype(jnp.float32).reshape(gathered_f32.shape)
        for fold in range(folds):
            x[part * per_piece + fold // per_step, :, pl.ds(fold % per_step * LANES, LANES)] = gathered_f32[
                pl.ds(fold, rows, stride=folds), :
            ].astype(jnp.bfloat16)

    def project(step):
        part, within = step // per_piece, lax.rem(step, per_piece)

        @pl.when(within == 0)
        def _():
            assemble(part)

        slot = lax.rem(step, slots)
        for half_of in range(2):
            weight_copy(step, half_of).wait()
        for half_of in range(parts):
            for column in range(0, width, TILE):
                stop = min(column + TILE, width)
                acc[half_of, :, column:stop] += jnp.dot(
                    x[step], ring[slot, half_of, :, column:stop], preferred_element_type=jnp.float32
                )

        @pl.when(step + slots < k_steps)
        def _():
            fill(step + slots)

        ahead = step + slots - k_steps

        @pl.when(jnp.logical_and(ahead >= 0, ahead < down_slots // fan))
        def _():
            for which in range(fan):
                down_copy(ahead * fan + which).start()

        @pl.when(jnp.logical_and(within == 0, part + 1 < pieces))
        def _():
            collect(part + 1)

    @pl.loop(0, pieces)
    def _(part):
        each(1, chips, functools.partial(announce, part))

    acc[...] = jnp.zeros_like(acc)
    collect(0)
    each(0, k_steps, project)
    each(min(slots, down_slots // fan) * fan, down_slots, lambda ahead: down_copy(ahead).start())

    if parts == 1:
        gate_out, up_out = acc[0, :, :units], acc[0, :, units:]
    else:
        gate_out, up_out = acc[0], acc[1]
    hidden[...] = (gate_out / (1.0 + jnp.exp(-gate_out)) * up_out).astype(jnp.bfloat16)

    def sibling(step):
        return pltpu.make_async_remote_copy(
            src_ref=sib_send.at[step],
            dst_ref=sib_recv.at[step],
            send_sem=sib_send_sem.at[step],
            recv_sem=sib_recv_sem.at[step],
            device_id=at(chip, other),
            device_id_type=MESH,
        )

    def produce(step):
        for sub in range(subs):
            chunk = step * subs + sub
            down_copy(chunk).wait()
            slot = lax.rem(chunk, down_slots)
            for column in range(0, D_CHUNK, TILE):
                product = jnp.dot(
                    hidden[...], down_ring[slot, :, column : column + TILE], preferred_element_type=jnp.float32
                )
                for lane in range(0, TILE, LANES):
                    fold = (sub * D_CHUNK + column + lane) // LANES
                    partial[pl.ds(fold, rows, stride=span), :] = product[:, lane : lane + LANES]

            @pl.when(chunk + down_slots < d_steps)
            def _():
                down_copy(chunk + down_slots).start()

            if sub == EARLY:
                pl.when(step >= 1)(lambda: exchange(step - 1))

        sib_send[step] = partial[pl.ds(pl.multiple_of(other * half, half), half), :].astype(jnp.bfloat16)
        mine[step] = partial[pl.ds(pl.multiple_of(core * half, half), half), :]
        sibling(step).start()

    def exchange(step):
        sibling(step).wait_recv()
        both = mine[step] + sib_recv[step].astype(jnp.float32)
        chip_send[step] = both.astype(jnp.bfloat16).reshape(chip_send.shape[1:])

        def send(ahead):
            to = peer(ahead)
            pltpu.make_async_remote_copy(
                src_ref=chip_send.at[step, to],
                dst_ref=chip_recv.at[step, chip],
                send_sem=chip_send_sem.at[step],
                recv_sem=chip_recv_sem.at[step],
                device_id=at(to, core),
                device_id_type=MESH,
            ).start()

        each(1, chips, send)
        chip_recv[step, chip] = chip_send[step, chip]

    def finish(step):
        whole_wait(chip_recv.at[step, pl.ds(0, chips - 1)], chip_recv_sem.at[step])
        total[...] = jnp.sum(chip_recv[step].astype(jnp.float32), axis=0)
        for fold in range(span):
            out_ref[:, pl.ds(pl.multiple_of(step * N_CHUNK, N_CHUNK) + fold * LANES, LANES)] = total[
                pl.ds(fold, own, stride=span), :
            ].astype(jnp.bfloat16)

    @pl.loop(0, n_steps + LAG)
    def _(step):
        pl.when(step < n_steps)(lambda: produce(step))
        pl.when(step == n_steps)(lambda: exchange(step - 1))
        pl.when(step >= LAG)(lambda: finish(step - LAG))

    @pl.loop(0, n_steps)
    def _(step):
        sibling(step).wait_send()
        whole_wait(chip_send.at[step, pl.ds(0, chips - 1)], chip_send_sem.at[step])

    @pl.loop(0, pieces)
    def _(part):
        forward(part).wait_send()
        whole_wait(gathered.at[core, part, pl.ds(0, chips - 1)], ag_send_sem)


def per_device(devices, tokens, norm_gain, gate_weight, up_weight, down_weight):
    own, features = tokens.shape
    units = gate_weight.shape[1]
    chips = devices // 2
    rows = devices * own
    folds = features // LANES // PIECES
    k_steps, n_steps = features // K_CHUNK, features // N_CHUNK
    slots, down_slots = min(RING, k_steps), min(DOWN_RING, features // D_CHUNK)
    parts = 1 if units % LANES == 0 else 2
    width = 2 * units // parts
    bf16, f32 = jnp.bfloat16, jnp.float32
    dma = pltpu.SemaphoreType.DMA
    span = N_CHUNK // LANES
    half = chips * own * span
    return pl.pallas_call(
        functools.partial(kernel, chips),
        out_shape=jax.ShapeDtypeStruct((own, features), bf16),
        in_specs=[pl.BlockSpec(memory_space=pl.ANY)] * 5,
        out_specs=pl.BlockSpec(memory_space=pltpu.VMEM),
        scratch_shapes=[
            pltpu.VMEM((own, features), bf16),
            pltpu.VMEM((1, features), f32),
            pltpu.VMEM((PIECES, own * folds, LANES), f32),
            pltpu.VMEM((PIECES, own * folds, LANES), bf16),
            pltpu.VMEM((2, PIECES, chips, own * folds, LANES), bf16),
            pltpu.VMEM((rows * folds, LANES), f32),
            pltpu.VMEM((k_steps, rows, K_CHUNK), bf16),
            pltpu.VMEM((slots, parts, K_CHUNK, width), bf16),
            pltpu.VMEM((down_slots, units, D_CHUNK), bf16),
            pltpu.VMEM((parts, rows, width), f32),
            pltpu.VMEM((rows, units), bf16),
            dma((2,)),
            dma((slots, 2)),
            dma((down_slots,)),
            dma,
            dma((PIECES,)),
            dma((PIECES,)),
            dma((PIECES,)),
            pltpu.VMEM((rows * span, LANES), f32),
            pltpu.VMEM((n_steps, half, LANES), f32),
            pltpu.VMEM((n_steps, half, LANES), bf16),
            pltpu.VMEM((n_steps, half, LANES), bf16),
            pltpu.VMEM((n_steps, chips, own * span, LANES), bf16),
            pltpu.VMEM((n_steps, chips, own * span, LANES), bf16),
            pltpu.VMEM((own * span, LANES), f32),
            dma((n_steps,)),
            dma((n_steps,)),
            dma((n_steps,)),
            dma((n_steps,)),
        ],
        compiler_params=pltpu.CompilerParams(
            collective_id=0, has_side_effects=True, vmem_limit_bytes=60 * 1024 * 1024
        ),
        cost_estimate=pl.CostEstimate(
            flops=6 * rows * features * units,
            bytes_accessed=6 * features * units,
            transcendentals=rows * units,
        ),
    )(tokens, norm_gain.reshape(1, features), gate_weight, up_weight, down_weight)


def solution(mesh):
    placed = (P(("groups", "row"), None), P(), P(None, "row"), P(None, "row"), P("row", None))
    return jax.shard_map(
        functools.partial(per_device, mesh.shape["row"]),
        mesh=mesh,
        in_specs=placed,
        out_specs=P(("groups", "row"), None),
        check_vma=False,
    )
```

time: 47.7 us -> 37.2 us (0.78)
  Pallas kernels: 46.1 us -> 35.6 us
    pallas_call x1, Pallas kernels: 46.1 us -> 35.6 us  [per_device(): pl.pallas_call(functools.partial(kernel, chips), out_shape=jax.ShapeDtype...]
where the time goes in v3:
time: 37.2 us; the launch traced here: 37 us
  Pallas kernels  35.6 us (96%)
  local copies, waits for them, and re-layouts  1.4 us (4%)
    pallas_call x1, Pallas kernels, per_device(): pl.pallas_call(functools.partial(kernel, chips), out_shape=jax.ShapeDtype...  35.6 us
    unnamed x1, local copies, waits for them, and re-layouts  1.4 us

profile of v3, /device:TPU:0, one launch (start us, length us, event | category | flops | bytes accessed | tf_op | source)
XLA Modules:
  0.0 37.0 jit_solution(2126113245042251875)
XLA Ops:
  0.0 35.6 %shard_map.55 = bf16[2,8192]{1,0:T(2,128)(2,1)} custom-call(bf16[2,8192]{1,0:T(2,128)(2,1)} %tokens_hbm.1, f32[1,8192]{1,0:T(1,128)} %bitcast.1, bf16[8192,1664]{1,0:T(8,128)(2,1)} %gate_hbm.1, bf16[8192,1664]{1,0:T(8,128)(2,1)} %up_hbm.1, bf16[1664,8192]{1,0:T(8,128)(2,1)} %down_hbm.1), custom_call_target="tpu_custom_call" | custom-call | flops 2617245696 | bytes 81788928 | tf_op jit(solution)/shard_map/pallas_call | solution.py:319
  35.6 1.4 %copy.7 = bf16[2,8192]{1,0:T(2,128)(2,1)} copy(bf16[2,8192]{1,0:T(2,128)(2,1)} %shard_map.55) | data formatting | bytes 65536
